TPU v7x, 256 devices: a whole 4x4x8 slice. The times are simulated.
256 devices in a mesh: dp: 4 (over x), context: 64 (over y, z, core).
Axes of the slice: x: 4, y: 4, z: 8, core: 2. Of those that a mesh axis runs over, the one named last changes fastest.
Arguments:
- queries: bfloat16 [32768, 8192], P(('dp', 'context')), parts along dimension 0, may hold values from -6 to 6
- out_grad: bfloat16 [32768, 8192], P(('dp', 'context')), parts along dimension 0, may hold values from -6 to 6
- image_keys: bfloat16 [4096, 1024], P(('dp', 'context')), parts along dimension 0, may hold values from -6 to 6
- image_values: bfloat16 [4096, 1024], P(('dp', 'context')), parts along dimension 0, may hold values from -6 to 6
- link_ids: int32 [16], P('dp'), parts along dimension 0, may hold values from 0 to 3, each once
- token_counts: int32 [16], P('dp'), parts along dimension 0, may hold values from 1 to 256, 640 in all
- tile_mask: int32 [256, 4], P('dp'), parts along dimension 0, may hold values from 0 to 1, as said below
Outputs:
- query_grad: bfloat16 [32768, 8192], P(('dp', 'context')), parts along dimension 0
- key_grad: float32 [4096, 1024], P(('dp', 'context')), parts along dimension 0
- value_grad: float32 [4096, 1024], P(('dp', 'context')), parts along dimension 0
There are 4 independent parts, one for each index of `dp`. A program takes and returns all parts, laid end to end along the dimension named above; each array names one. Nothing has to cross between parts.
Inputs may be any that keep to these rules, and one draw needn't show every extreme that they name: `link_ids`: a permutation of the stored images. `token_counts`: one image has all 256 slots live. tile_mask[t, p] = 1 exactly when t is at or past the start tile of link position p; position 0 starts at tile 0.
All inputs are finite; a program needn't handle non-finite values.
Results may differ from a plain program's by a relative error of at most 0.0066.
Values may be sent and summed in bfloat16 or wider, within the bound.
A program may use at most 192 MiB of HBM per device.

v0:
```python
import math

import jax
import jax.numpy as jnp
from jax import lax
from jax.sharding import PartitionSpec as P

H = 64
KVH = 8
HD = 128
TILE = 128
IMAGES = 4
VIS = 256


def link_table(link_ids, tile_mask):
    onehot = (link_ids[:, None] == jnp.arange(IMAGES, dtype=jnp.int32)[None, :]).astype(jnp.float32)
    return jnp.sum(tile_mask.astype(jnp.float32)[:, :, None] * onehot[None, :, :], axis=1)


def key_valid(token_counts):
    slots = jnp.arange(IMAGES * VIS, dtype=jnp.int32)
    owner = slots // VIS
    inside = slots - owner * VIS
    same = owner[None, :] == jnp.arange(IMAGES, dtype=jnp.int32)[:, None]
    live = inside[None, :] < token_counts[:, None]
    return (same & live).astype(jnp.float32)


def allowed_block(table, valid, row_start, rows):
    tiles = lax.dynamic_slice_in_dim(table, row_start // TILE, rows // TILE, 0)
    spread = jnp.repeat(tiles, TILE, axis=0)
    allowed = spread[:, 0:1] * valid[0][None, :]
    for image in range(1, IMAGES):
        allowed = allowed + spread[:, image : image + 1] * valid[image][None, :]
    return allowed


def group_backward(query_rows, grad_rows, key_head, value_head, allowed):
    score_scale = 1.0 / math.sqrt(HD)
    scores = (
        jnp.einsum("rgd,ld->grl", query_rows, key_head, preferred_element_type=jnp.float32)
        * score_scale
    )
    scores = jnp.where(allowed[None] > 0, scores, jnp.float32(-1e30))
    row_max = jnp.max(scores, axis=-1, keepdims=True)
    weights = jnp.exp(scores - row_max)
    probs = weights / jnp.sum(weights, axis=-1, keepdims=True)
    probs_low = probs.astype(jnp.bfloat16)
    dprobs = jnp.einsum("rgd,ld->grl", grad_rows, value_head, preferred_element_type=jnp.float32)
    row_delta = jnp.sum(probs * dprobs, axis=-1, keepdims=True)
    dscores = (probs * (dprobs - row_delta) * score_scale).astype(jnp.bfloat16)
    query_part = jnp.einsum("grl,ld->rgd", dscores, key_head, preferred_element_type=jnp.float32)
    key_part = jnp.einsum("grl,rgd->ld", dscores, query_rows, preferred_element_type=jnp.float32)
    value_part = jnp.einsum("grl,rgd->ld", probs_low, grad_rows, preferred_element_type=jnp.float32)
    return (query_part, key_part, value_part)


def heads_layout(queries, out_grad, image_keys, image_values, table, valid):
    count = lax.axis_size("context")
    heads_here = H // count
    kv_here = max(1, KVH // count)
    repeat_kv = max(1, count // KVH)
    per_kv = heads_here // kv_here
    own_rows = image_keys.shape[0]
    slots = own_rows * count
    text_q, text_g = (
        lax.all_to_all(queries, "context", split_axis=1, concat_axis=0, tiled=True),
        lax.all_to_all(out_grad, "context", split_axis=1, concat_axis=0, tiled=True),
    )
    send_keys = jnp.repeat(image_keys.reshape(own_rows, KVH, HD), repeat_kv, axis=1).reshape(
        own_rows, KVH * repeat_kv * HD
    )
    send_values = jnp.repeat(image_values.reshape(own_rows, KVH, HD), repeat_kv, axis=1).reshape(
        own_rows, KVH * repeat_kv * HD
    )
    my_keys, my_values = (
        lax.all_to_all(send_keys, "context", split_axis=1, concat_axis=0, tiled=True),
        lax.all_to_all(send_values, "context", split_axis=1, concat_axis=0, tiled=True),
    )
    total_rows = text_q.shape[0]
    block = math.gcd(total_rows, 512)

    def step(carry, start_block):
        key_acc, value_acc = carry
        row_start = start_block * block
        q_rows = lax.dynamic_slice_in_dim(text_q, row_start, block, 0)
        g_rows = lax.dynamic_slice_in_dim(text_g, row_start, block, 0)
        allowed = allowed_block(table, valid, row_start, block)
        query_parts, key_parts, value_parts = ([], [], [])
        q_blk = q_rows.reshape(block, per_kv, HD)
        g_blk = g_rows.reshape(block, per_kv, HD)
        query_part, key_part, value_part = group_backward(q_blk, g_blk, my_keys, my_values, allowed)
        query_parts.append(query_part.reshape(block, per_kv * HD))
        key_parts.append(key_part)
        value_parts.append(value_part)
        new_carry = (
            key_acc + jnp.concatenate(key_parts, axis=1),
            value_acc + jnp.concatenate(value_parts, axis=1),
        )
        return (new_carry, jnp.concatenate(query_parts, axis=1).astype(jnp.bfloat16))

    start = (
        jnp.zeros((slots, kv_here * HD), jnp.float32),
        jnp.zeros((slots, kv_here * HD), jnp.float32),
    )
    (key_terms, value_terms), blocks = lax.scan(
        step, start, jnp.arange(total_rows // block, dtype=jnp.int32)
    )
    query_grad = lax.all_to_all(
        blocks.reshape(total_rows, heads_here * HD),
        "context",
        split_axis=0,
        concat_axis=1,
        tiled=True,
    )
    got_keys, got_values = (
        lax.all_to_all(key_terms, "context", split_axis=0, concat_axis=1, tiled=True),
        lax.all_to_all(value_terms, "context", split_axis=0, concat_axis=1, tiled=True),
    )
    key_grad = jnp.sum(got_keys.reshape(own_rows, KVH, repeat_kv, HD), axis=2).reshape(
        own_rows, KVH * HD
    )
    value_grad = jnp.sum(got_values.reshape(own_rows, KVH, repeat_kv, HD), axis=2).reshape(
        own_rows, KVH * HD
    )
    return (query_grad, key_grad, value_grad)


def body(queries, out_grad, image_keys, image_values, link_ids, token_counts, tile_mask):
    table = link_table(link_ids, tile_mask)
    valid = key_valid(token_counts)
    return heads_layout(queries, out_grad, image_keys, image_values, table, valid)


def solution(mesh):
    return jax.shard_map(
        body,
        mesh=mesh,
        in_specs=(
            P(("dp", "context"), None),
            P(("dp", "context"), None),
            P(("dp", "context"), None),
            P(("dp", "context"), None),
            P("dp"),
            P("dp"),
            P("dp", None),
        ),
        out_specs=(
            P(("dp", "context"), None),
            P(("dp", "context"), None),
            P(("dp", "context"), None),
        ),
        check_vma=False,
    )
```

profile of v0, /device:TPU:1, one launch (start us, length us, event | category | flops | bytes accessed | tf_op | source)
XLA Modules:
  0.0 483.3 jit_solution(9596371486049991485)
XLA Ops:
  2.3 13.2 %all-to-all-start.1 = ((bf16[16,64,128]{2,0,1:T(8,128)(2,1)}), bf16[16,64,128]{2,0,1:T(8,128)(2,1)S(1)}, u32[]{:S(2)}, u32[]{:S(2)}) async-start(bf16[16,64,128]{2,0,1:T(8,128)(2,1)} %bitcast.2), calls=%async_computation.1 | async-start | bytes 524288 | tf_op jit(solution)/shard_map/all_to_all | solution.py:78
  16.2 11.2 %all-to-all-done.1 = bf16[16,64,128]{2,0,1:T(8,128)(2,1)S(1)} async-done(((bf16[16,64,128]{2,0,1:T(8,128)(2,1)}), bf16[16,64,128]{2,0,1:T(8,128)(2,1)S(1)}, u32[]{:S(2)}, u32[]{:S(2)}) %all-to-all-start.1) | async-done | bytes 262176 | tf_op jit(solution)/shard_map/all_to_all | solution.py:78
  28.2 6.2 %all-to-all-start.3 = ((bf16[16,64,128]{2,0,1:T(8,128)(2,1)}), bf16[16,64,128]{2,0,1:T(8,128)(2,1)}, u32[]{:S(2)}, u32[]{:S(2)}) async-start(bf16[16,64,128]{2,0,1:T(8,128)(2,1)} %bitcast.7), calls=%async_computation.3 | async-start | bytes 524288 | tf_op jit(solution)/shard_map/all_to_all | solution.py:79
  34.4 1.9 copy_bitcast_fusion.2
  36.3 10.0 %all-to-all-done.3 = bf16[16,64,128]{2,0,1:T(8,128)(2,1)} async-done(((bf16[16,64,128]{2,0,1:T(8,128)(2,1)}), bf16[16,64,128]{2,0,1:T(8,128)(2,1)}, u32[]{:S(2)}, u32[]{:S(2)}) %all-to-all-start.3) | async-done | bytes 262176 | tf_op jit(solution)/shard_map/all_to_all | solution.py:79
  46.3 6.2 %all-to-all-start = ((bf16[128,64,128]{2,0,1:T(8,128)(2,1)}), bf16[128,64,128]{2,0,1:T(8,128)(2,1)}, u32[]{:S(2)}, u32[]{:S(2)}) async-start(bf16[128,64,128]{2,0,1:T(8,128)(2,1)} %copy_bitcast_fusion.2), calls=%async_computation | async-start | bytes 4194304 | tf_op jit(solution)/shard_map/all_to_all | solution.py:68
  52.6 3.5 copy_bitcast_fusion.1
  56.1 47.7 %all-to-all-done = bf16[128,64,128]{2,0,1:T(8,128)(2,1)} async-done(((bf16[128,64,128]{2,0,1:T(8,128)(2,1)}), bf16[128,64,128]{2,0,1:T(8,128)(2,1)}, u32[]{:S(2)}, u32[]{:S(2)}) %all-to-all-start) | async-done | bytes 2097184 | tf_op jit(solution)/shard_map/all_to_all | solution.py:68
  103.7 6.0 %all-to-all-start.2 = ((bf16[128,64,128]{2,0,1:T(8,128)(2,1)}), bf16[128,64,128]{2,0,1:T(8,128)(2,1)}, u32[]{:S(2)}, u32[]{:S(2)}) async-start(bf16[128,64,128]{2,0,1:T(8,128)(2,1)} %copy_bitcast_fusion.1), calls=%async_computation.2 | async-start | bytes 4194304 | tf_op jit(solution)/shard_map/all_to_all | solution.py:69
  110.0 50.9 %all-to-all-done.2 = bf16[128,64,128]{2,0,1:T(8,128)(2,1)} async-done(((bf16[128,64,128]{2,0,1:T(8,128)(2,1)}), bf16[128,64,128]{2,0,1:T(8,128)(2,1)}, u32[]{:S(2)}, u32[]{:S(2)}) %all-to-all-start.2) | async-done | bytes 2097184 | tf_op jit(solution)/shard_map/all_to_all | solution.py:69
  160.9 209.8 %while.17 = (s32[]{:T(128)}, f32[1024,128]{1,0:T(8,128)}, f32[1024,128]{1,0:T(8,128)}, bf16[16,512,128]{2,1,0:T(8,128)(2,1)}, s32[16]{0:T(128)S(1)}, /*index=5*/...) while((s32[]{:T(128)}, f32[1024,128]{1,0:T(8,128)}, ...), condition=%wide.region_5.6_spmd.clone, body=%wide.region_1.5_spmd.clone.sunk | while | flops 685308416 | bytes 29875344 | solution.py:107
  162.4 1.9 fusion.66
  168.4 3.1 convolution_add_fusion.5
  171.5 2.2 convolution_add_fusion.4
  175.2 1.9 fusion.66
  181.2 3.2 convolution_add_fusion.5
  184.4 2.4 convolution_add_fusion.4
  188.3 1.9 fusion.66
  194.3 3.2 convolution_add_fusion.5
  197.6 2.4 convolution_add_fusion.4
  201.4 1.9 fusion.66
  207.5 3.2 convolution_add_fusion.5
  210.7 2.4 convolution_add_fusion.4
  214.6 1.9 fusion.66
  220.6 3.2 convolution_add_fusion.5
  223.8 2.4 convolution_add_fusion.4
  227.7 1.9 fusion.66
  233.8 3.2 convolution_add_fusion.5
  237.0 2.4 convolution_add_fusion.4
  240.8 1.9 fusion.66
  246.9 3.2 convolution_add_fusion.5
  250.1 2.4 convolution_add_fusion.4
  254.0 1.9 fusion.66
  260.0 3.2 convolution_add_fusion.5
  263.3 2.4 convolution_add_fusion.4
  267.1 1.9 fusion.66
  273.2 3.2 convolution_add_fusion.5
  276.4 2.4 convolution_add_fusion.4
  280.2 1.9 fusion.66
  286.3 3.2 convolution_add_fusion.5
  289.5 2.4 convolution_add_fusion.4
  293.4 1.9 fusion.66
  299.4 3.2 convolution_add_fusion.5
  302.7 2.4 convolution_add_fusion.4
  306.5 1.9 fusion.66
  312.6 3.2 convolution_add_fusion.5
  315.8 2.4 convolution_add_fusion.4
  319.7 1.9 fusion.66
  325.7 3.2 convolution_add_fusion.5
  328.9 2.4 convolution_add_fusion.4
  332.8 1.9 fusion.66
  338.8 3.2 convolution_add_fusion.5
  342.1 2.4 convolution_add_fusion.4
  345.9 1.9 fusion.66
  352.0 3.2 convolution_add_fusion.5
  355.2 2.4 convolution_add_fusion.4
  365.1 3.2 convolution_add_fusion.5
  368.4 2.4 convolution_add_fusion.4
  370.7 23.1 %all_to_all.127 = f32[64,16,128]{2,1,0:T(8,128)S(1)} all-to-all(f32[64,16,128]{2,1,0:T(8,128)} %bitcast.162), channel_id=1, replica_groups=mesh['dp'=4,'context'=64] {'context'}, dimensions={0} | all-to-all | bytes 1048576 | tf_op jit(solution)/shard_map/all_to_all | solution.py:119
  393.9 23.6 %all_to_all.128 = f32[64,16,128]{2,1,0:T(8,128)S(1)} all-to-all(f32[64,16,128]{2,1,0:T(8,128)} %bitcast.13), channel_id=1, replica_groups=mesh['dp'=4,'context'=64] {'context'}, dimensions={0} | all-to-all | bytes 1048576 | tf_op jit(solution)/shard_map/all_to_all | solution.py:118
  417.5 6.5 %all-to-all-start.4 = ((bf16[64,128,128]{2,1,0:T(8,128)(2,1)}), bf16[64,128,128]{2,1,0:T(8,128)(2,1)}, u32[]{:S(2)}, u32[]{:S(2)}) async-start(bf16[64,128,128]{2,1,0:T(8,128)(2,1)} %bitcast.10), calls=%async_computation.4 | async-start | bytes 4194304 | tf_op jit(solution)/shard_map/all_to_all | solution.py:110
  425.3 49.8 %all-to-all-done.4 = bf16[64,128,128]{2,1,0:T(8,128)(2,1)} async-done(((bf16[64,128,128]{2,1,0:T(8,128)(2,1)}), bf16[64,128,128]{2,1,0:T(8,128)(2,1)}, u32[]{:S(2)}, u32[]{:S(2)}) %all-to-all-start.4) | async-done | bytes 2097184 | tf_op jit(solution)/shard_map/all_to_all | solution.py:110
  475.1 4.1 copy.41
  479.2 4.1 copy.44
  (218 shorter events, 85.0 us)
Async XLA Ops:
  0.6 33.8 %copy-start = (bf16[128,8192]{1,0:T(8,128)(2,1)S(1)}, bf16[128,8192]{1,0:T(8,128)(2,1)}, u32[]{:S(2)}) copy-start(bf16[128,8192]{1,0:T(8,128)(2,1)} %param.9) | copy-start | bytes 6291460
  2.3 25.2 %all-to-all-start.1 = ((bf16[16,64,128]{2,0,1:T(8,128)(2,1)}), bf16[16,64,128]{2,0,1:T(8,128)(2,1)S(1)}, u32[]{:S(2)}, u32[]{:S(2)}) async-start(bf16[16,64,128]{2,0,1:T(8,128)(2,1)} %bitcast.2), calls=%async_computation.1 | async-start | bytes 524288 | tf_op jit(solution)/shard_map/all_to_all | solution.py:78
  28.2 18.1 %all-to-all-start.3 = ((bf16[16,64,128]{2,0,1:T(8,128)(2,1)}), bf16[16,64,128]{2,0,1:T(8,128)(2,1)}, u32[]{:S(2)}, u32[]{:S(2)}) async-start(bf16[16,64,128]{2,0,1:T(8,128)(2,1)} %bitcast.7), calls=%async_computation.3 | async-start | bytes 524288 | tf_op jit(solution)/shard_map/all_to_all | solution.py:79
  46.3 57.4 %all-to-all-start = ((bf16[128,64,128]{2,0,1:T(8,128)(2,1)}), bf16[128,64,128]{2,0,1:T(8,128)(2,1)}, u32[]{:S(2)}, u32[]{:S(2)}) async-start(bf16[128,64,128]{2,0,1:T(8,128)(2,1)} %copy_bitcast_fusion.2), calls=%async_computation | async-start | bytes 4194304 | tf_op jit(solution)/shard_map/all_to_all | solution.py:68
  56.0 53.7 %copy-start.2 = (s32[64,4]{0,1:T(4,128)S(1)}, s32[64,4]{0,1:T(4,128)}, u32[]{:S(2)}) copy-start(s32[64,4]{0,1:T(4,128)} %param.15) | copy-start | bytes 3076
  56.1 53.7 %copy-start.3 = (s32[4]{0:T(128)S(1)}, s32[4]{0:T(128)}, u32[]{:S(2)}) copy-start(s32[4]{0:T(128)} %param.13) | copy-start | bytes 52
  56.1 53.9 %copy-start.4 = (s32[4]{0:T(128)S(1)}, s32[4]{0:T(128)}, u32[]{:S(2)}) copy-start(s32[4]{0:T(128)} %param.14) | copy-start | bytes 52
  103.7 57.2 %all-to-all-start.2 = ((bf16[128,64,128]{2,0,1:T(8,128)(2,1)}), bf16[128,64,128]{2,0,1:T(8,128)(2,1)}, u32[]{:S(2)}, u32[]{:S(2)}) async-start(bf16[128,64,128]{2,0,1:T(8,128)(2,1)} %copy_bitcast_fusion.1), calls=%async_computation.2 | async-start | bytes 4194304 | tf_op jit(solution)/shard_map/all_to_all | solution.py:69
  164.3 2.4 copy-start.1
  177.1 2.4 copy-start.1
  190.2 2.4 copy-start.1
  203.3 2.4 copy-start.1
  216.5 2.4 copy-start.1
  229.6 2.4 copy-start.1
  242.7 2.4 copy-start.1
  255.9 2.4 copy-start.1
  269.0 2.4 copy-start.1
  282.1 2.4 copy-start.1
  295.3 2.4 copy-start.1
  308.4 2.4 copy-start.1
  321.6 2.4 copy-start.1
  334.7 2.4 copy-start.1
  347.8 2.4 copy-start.1
  361.0 2.4 copy-start.1
  417.5 57.6 %all-to-all-start.4 = ((bf16[64,128,128]{2,1,0:T(8,128)(2,1)}), bf16[64,128,128]{2,1,0:T(8,128)(2,1)}, u32[]{:S(2)}, u32[]{:S(2)}) async-start(bf16[64,128,128]{2,1,0:T(8,128)(2,1)} %bitcast.10), calls=%async_computation.4 | async-start | bytes 4194304 | tf_op jit(solution)/shard_map/all_to_all | solution.py:110
where the time goes:
time: 486 us; the launch traced here: 483 us
  waiting for transfers between devices  170 us (35%)
  matrix products  168 us (35%)
  blocking collectives  46.7 us (10%)
  starting transfers between devices  38.1 us (8%)
  local copies, waits for them, and re-layouts  30.2 us (6%)
  other arithmetic  18.5 us (4%)
  loops' own time  11.6 us (2%)
    dot_general x16, matrix products, group_backward(): jnp.einsum('grl,rgd->ld', probs_low, grad_rows, preferred_element_type=jn...  51.6 us
    all_to_all x1, waiting for transfers between devices, heads_layout(): lax.all_to_all(out_grad, 'context', split_axis=1, concat_axis=0, tiled=True)  50.9 us
    all_to_all x1, waiting for transfers between devices, heads_layout(): lax.all_to_all(blocks.reshape(total_rows, heads_here * HD), 'context', sp...  49.8 us
    all_to_all x1, waiting for transfers between devices, heads_layout(): lax.all_to_all(queries, 'context', split_axis=1, concat_axis=0, tiled=True)  47.7 us
    dot_general x16, matrix products, group_backward(): jnp.einsum('grl,rgd->ld', dscores, query_rows, preferred_element_type=jnp...  37.9 us
    dot_general x16, matrix products, group_backward(): jnp.einsum('rgd,ld->grl', query_rows, key_head, preferred_element_type=jn...  30.4 us
    dot_general x16, matrix products, group_backward(): jnp.einsum('rgd,ld->grl', grad_rows, value_head, preferred_element_type=j...  30.3 us
    all_to_all x1, blocking collectives, heads_layout(): lax.all_to_all(key_terms, 'context', split_axis=0, concat_axis=1, tiled=T...  23.6 us
  transfers between devices with their start and end apart: 5, of which 5 were waited for; matrix products, arithmetic and copies ran while one was open for 2% of the time, Pallas kernels for 0%

commit v1 on v0

v1 whole, which is shorter than its diff:
```python
import functools
import math

import jax
import jax.numpy as jnp
from jax import lax
from jax.experimental import pallas as pl
from jax.experimental.pallas import tpu as pltpu
from jax.sharding import PartitionSpec as P

H = 64
KVH = 8
HD = 128
TILE = 128
IMAGES = 4
VIS = 256
GROUP = H // KVH
PAIRS = GROUP // 2
NY = 4
NZ = 8
ROWS = 16
BLOCKS = IMAGES * VIS // ROWS
LIVE = 42
L = LIVE * ROWS
CHUNK = 112
SCALE = 1.0 / math.sqrt(HD)
SCALE2 = SCALE * math.log2(math.e)
NEG = -1e30
Z_GROUPS = ((0, 1), (1, 3), (4, 4))
MESH = pl.DeviceIdType.MESH
f32 = jnp.float32
bf16 = jnp.bfloat16


def dot(a, b, ca, cb):
    return lax.dot_general(a, b, (((ca,), (cb,)), ((), ())), preferred_element_type=f32)


def device(y, z, k):
    return {"context": (y * NZ + z) * 2 + k}


def remote(src, dst, sems, at, target):
    send, recv = sems
    return pltpu.make_async_remote_copy(
        src_ref=src,
        dst_ref=dst,
        send_sem=send.at[at],
        recv_sem=recv.at[at],
        device_id=target,
        device_id_type=MESH,
    )


def kernel(
    links, counts, tiles, q_hbm, g_hbm, k_in, v_in,
    dq_hbm, dk_out, dv_out,
    q, g, dq, kv, cur, kaug, vc, kt, s0, s1, d0, d1, e_buf, p0, p1, w0, w1, dk_acc, dv_acc,
    rs_full, rs_sib, rs_y, rs_yr, rs_z, rs_zr, src_tbl, dst_tbl, row_tbl,
    load_sem, dq_sem, zs, zr, ys, yr, cs, cr, rcs, rcr, rys, ryr, rzs, rzr,
):
    c = lax.axis_index("context")
    y, z, k = c // (2 * NZ), lax.rem(c // 2, NZ), lax.rem(c, 2)
    other = 1 - k
    yy = [lax.rem(y + d, NY) for d in range(NY)]
    zz = [lax.rem(z + d, NZ) for d in range(NZ)]
    sibling = device(y, z, other)
    y_peer = [device(yy[d], z, k) for d in range(NY)]
    z_peer = [device(y, zz[d], k) for d in range(NZ)]
    z_sem, y_sem, c_sem = (zs, zr), (ys, yr), (cs, cr)
    rc_sem, ry_sem, rz_sem = (rcs, rcr), (rys, ryr), (rzs, rzr)

    q_load = pltpu.make_async_copy(q_hbm, q, load_sem.at[0])
    g_load = pltpu.make_async_copy(g_hbm, g, load_sem.at[1])
    q_load.start()
    g_load.start()

    barrier = pltpu.get_barrier_semaphore()
    peers = [sibling] + y_peer[1:] + z_peer[1:]
    for peer in peers:
        pl.semaphore_signal(barrier, inc=1, device_id=peer, device_id_type=MESH)
    for h in range(KVH):
        kv[h, k, y, z, 0] = k_in[:, h * HD : (h + 1) * HD]
        kv[h, k, y, z, 1] = v_in[:, h * HD : (h + 1) * HD]
    pl.semaphore_wait(barrier, len(peers))

    def z_send(group, d):
        heads = pl.ds(*Z_GROUPS[group])
        mine = kv.at[heads, k, y, z]
        return remote(mine, mine, z_sem, (group, d - 1), z_peer[d])

    def z_recv(group, d):
        heads = pl.ds(*Z_GROUPS[group])
        return remote(kv.at[heads, k, y, z], kv.at[heads, k, y, zz[NZ - d]], z_sem, (group, d - 1), z_peer[d])

    def y_send(h, d):
        return remote(kv.at[h, k, y], kv.at[h, k, y], y_sem, (h, d - 1), y_peer[d])

    def y_recv(h, d):
        return remote(kv.at[h, k, y], kv.at[h, k, yy[NY - d]], y_sem, (h, d - 1), y_peer[d])

    def c_send(h):
        return remote(kv.at[h, k], kv.at[h, k], c_sem, (h,), sibling)

    def c_recv(h):
        return remote(kv.at[h, k], kv.at[h, other], c_sem, (h,), sibling)

    for group in range(len(Z_GROUPS)):
        for d in range(1, NZ):
            z_send(group, d).start()

    def pass_on(group):
        for d in range(1, NZ):
            z_recv(group, d).wait_recv()
        first, number = Z_GROUPS[group]
        for h in range(first, first + number):
            for d in range(1, NY):
                y_send(h, d).start()

    pass_on(0)

    zero = jnp.int32(0)
    live_rows, first_block = [], [zero]
    for image in range(IMAGES):
        seen = zero
        for p in range(IMAGES):
            seen = seen + jnp.where(links[p] == image, tiles[c, p], 0)
        live_rows.append(jnp.where(seen > 0, counts[image], 0))
        first_block.append(first_block[-1] + (live_rows[-1] + (ROWS - 1)) // ROWS)
    spare = first_block[IMAGES]

    def fill_src(b, _):
        image, base, rows = zero, zero, live_rows[0]
        for i in range(1, IMAGES):
            past = b >= first_block[i]
            image = jnp.where(past, i, image)
            base = jnp.where(past, first_block[i], base)
            rows = jnp.where(past, live_rows[i], rows)
        u = jnp.minimum(b - base, VIS // ROWS - 1)
        src_tbl[b] = lax.rem(u, 2) * (NY * NZ) + image * NZ + u // 2
        row_tbl[b] = jnp.where(b < spare, rows - (b - base) * ROWS, 0)
        return 0

    lax.fori_loop(0, LIVE, fill_src, 0)
    for image in range(IMAGES):

        def fill_dst(u, _):
            at = lax.rem(u, 2) * (NY * NZ) + image * NZ + u // 2
            dst_tbl[at] = jnp.where(u * ROWS < live_rows[image], first_block[image] + u, LIVE)
            return 0

        lax.fori_loop(0, VIS // ROWS, fill_dst, 0)

    lane = lax.broadcasted_iota(jnp.int32, (ROWS, HD), 1)
    row = lax.broadcasted_iota(jnp.int32, (ROWS, HD), 0)

    def fill_bias(b, _):
        dead = jnp.logical_and(lane == 0, row >= row_tbl[b])
        kaug[b, :, HD:] = jnp.where(dead, NEG, 0.0).astype(bf16)
        return 0

    lax.fori_loop(0, LIVE, fill_bias, 0)
    dk_acc[LIVE] = jnp.zeros((ROWS, HD), f32)
    dv_acc[LIVE] = jnp.zeros((ROWS, HD), f32)

    def compact(h):
        flat = 2 * NY * NZ
        cur[...] = kv[h].reshape(flat, 2, ROWS, HD)
        for b in range(LIVE):
            kaug[b, :, :HD] = cur[src_tbl[b], 0]
            vc[b] = cur[src_tbl[b], 1]

    def transpose_keys():
        kt[...] = kaug[...].reshape(L, 2 * HD)[:, :HD].T

    s_buf, d_buf, p_buf, w_buf = (s0, s1), (d0, d1), (p0, p1), (w0, w1)
    ones = jnp.where(lax.broadcasted_iota(jnp.int32, (2 * TILE, HD), 1) == 0, 1.0, 0.0).astype(bf16)

    def two_heads(ref, h, pair):
        start = pl.multiple_of(h * (GROUP * HD) + pair * (2 * HD), 2 * HD)
        both = ref[:, pl.ds(start, 2 * HD)]
        return jnp.concatenate([both[:, :HD], both[:, HD:]], axis=0)

    def front(h, pair, slot):
        rows_q = jnp.concatenate([two_heads(q, h, pair), ones], axis=1)
        s_buf[slot][...] = dot(kaug[...].reshape(L, 2 * HD), rows_q, 1, 1)
        d_buf[slot][...] = dot(vc[...].reshape(L, HD), two_heads(g, h, pair), 1, 1)

    def middle(slot):
        tops, sums, deltas = [], [], []
        lanes = 2 * TILE
        for i in range(L // CHUNK):
            at = slice(i * CHUNK, (i + 1) * CHUNK)
            s = s_buf[slot][at, :]
            top = jnp.max(s, axis=0, keepdims=True) * SCALE2
            e = jnp.exp2(s * SCALE2 - top)
            e_buf[at, :] = e
            sums.append(jnp.sum(e.reshape(CHUNK // 8, 8, lanes), axis=0))
            deltas.append(jnp.sum((e * d_buf[slot][at, :]).reshape(CHUNK // 8, 8, lanes), axis=0))
            tops.append(top)
        top = functools.reduce(jnp.maximum, tops)
        weight = [jnp.exp2(t - top) for t in tops]
        total = jnp.sum(sum(a * b for a, b in zip(sums, weight)), axis=0, keepdims=True)
        delta = jnp.sum(sum(a * b for a, b in zip(deltas, weight)), axis=0, keepdims=True)
        inverse = 1.0 / total
        delta = delta * inverse
        for i in range(L // CHUNK):
            at = slice(i * CHUNK, (i + 1) * CHUNK)
            prob = e_buf[at, :] * (weight[i] * inverse)
            p_buf[slot][at, :] = prob.astype(bf16)
            w_buf[slot][at, :] = (prob * (d_buf[slot][at, :] - delta)).astype(bf16)

    def back(h, pair, slot, first):
        dqt = dot(kt[...], w_buf[slot][...], 1, 0) * SCALE
        for j in range(2):
            start = pl.multiple_of(h * (GROUP * HD) + pair * (2 * HD) + j * HD, HD)
            dq[:, pl.ds(start, HD)] = dqt[:, j * TILE : (j + 1) * TILE].T.astype(bf16)
        dv = dot(p_buf[slot][...], two_heads(g, h, pair), 1, 0).reshape(LIVE, ROWS, HD)
        dk = dot(w_buf[slot][...], two_heads(q, h, pair), 1, 0).reshape(LIVE, ROWS, HD)
        if first:
            dv_acc[:LIVE] = dv
            dk_acc[:LIVE] = dk
        else:
            dv_acc[:LIVE] += dv
            dk_acc[:LIVE] += dk

    def rc_send(h):
        return remote(rs_full.at[h, other], rs_sib.at[h], rc_sem, (h,), sibling)

    def ry_send(h, d):
        return remote(rs_y.at[h, yy[d]], rs_yr.at[h, d - 1], ry_sem, (h, d - 1), y_peer[d])

    def rz_send(h, d):
        return remote(rs_z.at[h, zz[d]], rs_zr.at[h, d - 1], rz_sem, (h, d - 1), z_peer[d])

    def dq_store(h):
        cols = pl.ds(pl.multiple_of(h * (GROUP * HD), GROUP * HD), GROUP * HD)
        return pltpu.make_async_copy(dq.at[:, cols], dq_hbm.at[:, cols], dq_sem.at[h])

    def finish(h):
        for plane in range(2):
            for a in range(NY):
                for b in range(NZ):
                    at = dst_tbl[plane * (NY * NZ) + a * NZ + b]
                    rs_full[h, plane, a, b, 0] = (dk_acc[at] * SCALE).astype(bf16)
                    rs_full[h, plane, a, b, 1] = dv_acc[at].astype(bf16)
        rc_send(h).start()
        dq_store(h).start()

    def reduce_core(h):
        rc_send(h).wait_recv()
        for a in range(NY):
            rs_y[h, a] = (rs_full[h, k, a].astype(f32) + rs_sib[h, a].astype(f32)).astype(bf16)
        for d in range(1, NY):
            ry_send(h, d).start()

    def reduce_y(h):
        total = rs_y[h, y].astype(f32)
        for d in range(1, NY):
            ry_send(h, d).wait_recv()
            total = total + rs_yr[h, d - 1].astype(f32)
        rs_z[h] = total.astype(bf16)
        for d in range(1, NZ):
            rz_send(h, d).start()

    def reduce_z(h):
        total = rs_z[h, z].astype(f32)
        for d in range(1, NZ):
            rz_send(h, d).wait_recv()
            total = total + rs_zr[h, d - 1].astype(f32)
        cols = pl.ds(pl.multiple_of(h * HD, HD), HD)
        dk_out[:, cols] = total[0]
        dv_out[:, cols] = total[1]

    def bring(h):
        for d in range(1, NY):
            y_recv(h, d).wait_recv()
        c_send(h).start()

    bring(0)
    pass_on(1)
    c_recv(0).wait_recv()
    compact(0)
    q_load.wait()
    g_load.wait()
    front(0, 0, 0)

    def step(h, _):
        front(h, 1, 1)
        middle(0)

        @pl.when(h == 0)
        def _():
            pass_on(2)

        @pl.when(h > 0)
        def _():
            back(h - 1, 3, 1, False)
            finish(h - 1)

        @pl.when(h < KVH - 1)
        def _():
            bring(h + 1)

        transpose_keys()
        front(h, 2, 0)
        middle(1)
        back(h, 0, 0, True)

        @pl.when(h >= 1)
        def _():
            reduce_core(h - 1)

        front(h, 3, 1)
        middle(0)
        back(h, 1, 1, False)

        @pl.when(h >= 3)
        def _():
            reduce_y(h - 3)

        @pl.when(h >= 5)
        def _():
            reduce_z(h - 5)

        @pl.when(h < KVH - 1)
        def _():
            c_recv(h + 1).wait_recv()
            compact(h + 1)

        front(jnp.minimum(h + 1, KVH - 1), 0, 0)
        middle(1)
        back(h, 2, 0, False)
        return 0

    lax.fori_loop(0, KVH, step, 0)
    back(KVH - 1, 3, 1, False)
    finish(KVH - 1)
    reduce_y(KVH - 3)
    reduce_z(KVH - 5)
    reduce_core(KVH - 1)
    reduce_y(KVH - 2)
    reduce_z(KVH - 4)
    reduce_y(KVH - 1)
    reduce_z(KVH - 3)
    reduce_z(KVH - 2)
    reduce_z(KVH - 1)

    for group in range(len(Z_GROUPS)):
        for d in range(1, NZ):
            z_send(group, d).wait_send()

    def drain(h, _):
        for d in range(1, NY):
            y_send(h, d).wait_send()
            ry_send(h, d).wait_send()
        for d in range(1, NZ):
            rz_send(h, d).wait_send()
        c_send(h).wait_send()
        rc_send(h).wait_send()
        dq_store(h).wait()
        return 0

    lax.fori_loop(0, KVH, drain, 0)


def body(queries, out_grad, image_keys, image_values, link_ids, token_counts, tile_mask):
    smem = pl.BlockSpec(memory_space=pltpu.SMEM)
    vmem = pl.BlockSpec(memory_space=pltpu.VMEM)
    hbm = pl.BlockSpec(memory_space=pl.ANY)
    dma = pltpu.SemaphoreType.DMA
    lanes = 2 * TILE
    scratch = [
        pltpu.VMEM((TILE, H * HD), bf16),
        pltpu.VMEM((TILE, H * HD), bf16),
        pltpu.VMEM((TILE, H * HD), bf16),
        pltpu.VMEM((KVH, 2, NY, NZ, 2, ROWS, HD), bf16),
        pltpu.VMEM((BLOCKS, 2, ROWS, HD), bf16),
        pltpu.VMEM((LIVE, ROWS, 2 * HD), bf16),
        pltpu.VMEM((LIVE, ROWS, HD), bf16),
        pltpu.VMEM((HD, L), bf16),
        pltpu.VMEM((L, lanes), f32),
        pltpu.VMEM((L, lanes), f32),
        pltpu.VMEM((L, lanes), f32),
        pltpu.VMEM((L, lanes), f32),
        pltpu.VMEM((L, lanes), f32),
        pltpu.VMEM((L, lanes), bf16),
        pltpu.VMEM((L, lanes), bf16),
        pltpu.VMEM((L, lanes), bf16),
        pltpu.VMEM((L, lanes), bf16),
        pltpu.VMEM((LIVE + 1, ROWS, HD), f32),
        pltpu.VMEM((LIVE + 1, ROWS, HD), f32),
        pltpu.VMEM((KVH, 2, NY, NZ, 2, ROWS, HD), bf16),
        pltpu.VMEM((KVH, NY, NZ, 2, ROWS, HD), bf16),
        pltpu.VMEM((KVH, NY, NZ, 2, ROWS, HD), bf16),
        pltpu.VMEM((KVH, NY - 1, NZ, 2, ROWS, HD), bf16),
        pltpu.VMEM((KVH, NZ, 2, ROWS, HD), bf16),
        pltpu.VMEM((KVH, NZ - 1, 2, ROWS, HD), bf16),
        pltpu.SMEM((LIVE,), jnp.int32),
        pltpu.SMEM((BLOCKS,), jnp.int32),
        pltpu.SMEM((LIVE,), jnp.int32),
        dma((2,)),
        dma((KVH,)),
        dma((len(Z_GROUPS), NZ - 1)),
        dma((len(Z_GROUPS), NZ - 1)),
        dma((KVH, NY - 1)),
        dma((KVH, NY - 1)),
        dma((KVH,)),
        dma((KVH,)),
        dma((KVH,)),
        dma((KVH,)),
        dma((KVH, NY - 1)),
        dma((KVH, NY - 1)),
        dma((KVH, NZ - 1)),
        dma((KVH, NZ - 1)),
    ]
    return pl.pallas_call(
        kernel,
        out_shape=(
            jax.ShapeDtypeStruct((TILE, H * HD), bf16),
            jax.ShapeDtypeStruct((ROWS, KVH * HD), f32),
            jax.ShapeDtypeStruct((ROWS, KVH * HD), f32),
        ),
        in_specs=[smem, smem, smem, hbm, hbm, vmem, vmem],
        out_specs=[hbm, vmem, vmem],
        scratch_shapes=scratch,
        compiler_params=pltpu.CompilerParams(
            collective_id=0, has_side_effects=True, vmem_limit_bytes=56 << 20
        ),
        cost_estimate=pl.CostEstimate(
            flops=5 * 2 * TILE * H * L * HD, bytes_accessed=8 << 20, transcendentals=TILE * H * L
        ),
    )(link_ids, token_counts, tile_mask, queries, out_grad, image_keys, image_values)


def solution(mesh):
    rows = P(("dp", "context"), None)
    return jax.shard_map(
        body,
        mesh=mesh,
        in_specs=(rows, rows, rows, rows, P("dp"), P("dp"), P("dp", None)),
        out_specs=(rows, rows, rows),
        check_vma=False,
    )
```

time: 486 us -> 85.2 us (0.18)
  waiting for transfers between devices: 170 us -> 0 us
  matrix products: 168 us -> 0 us
  Pallas kernels: 0 us -> 78.5 us
  blocking collectives: 46.7 us -> 0 us
  starting transfers between devices: 38.1 us -> 0 us
  local copies, waits for them, and re-layouts: 30.2 us -> 5.78 us
  other arithmetic: 18.5 us -> 0 us
  loops' own time: 11.6 us -> 0 us
    all_to_all x5 -> x0, waiting for transfers between devices: 170 us -> none  [the longest x1 50.9 us: heads_layout(): lax.all_to_all(out_grad, 'context', split_axis=1, concat_axis=0, tiled=True)]
    dot_general x80 -> x0, matrix products: 168 us -> none  [the longest x16 51.6 us: group_backward(): jnp.einsum('grl,rgd->ld', probs_low, grad_rows, preferred_element_type=jn...]
    pallas_call x0 -> x1, Pallas kernels: none -> 78.5 us  [body(): pl.pallas_call(kernel, out_shape=(jax.ShapeDtypeStruct((TILE, H * HD), bf...]
    all_to_all x2 -> x0, blocking collectives: 46.7 us -> none  [the longest x1 23.6 us: heads_layout(): lax.all_to_all(key_terms, 'context', split_axis=0, concat_axis=1, tiled=T...]
    all_to_all x5 -> x0, starting transfers between devices: 38.1 us -> none  [the longest x1 13.2 us: heads_layout(): lax.all_to_all(send_keys, 'context', split_axis=1, concat_axis=0, tiled=T...]
    another operation x1 -> x0, loops' own time: 11.6 us -> none  [heads_layout(): lax.scan(step, start, jnp.arange(total_rows // block, dtype=jnp.int32))]
    dynamic_slice x32 -> x0, local copies, waits for them, and re-layouts: 10.5 us -> none  [the longest x16 9.32 us: heads_layout(): lax.scan(step, start, jnp.arange(total_rows // block, dtype=jnp.int32))]
    another operation x16 -> x0, other arithmetic: 10.1 us -> none
  transfers between devices with their start and end apart: 5 -> 0, of which waited for: 5 -> 0; matrix products, arithmetic and copies ran while one was open for 2% -> 0% of each run, Pallas kernels for 0% -> 0%
where the time goes in v1:
time: 85.2 us; the launch traced here: 85 us
  Pallas kernels  78.5 us (92%)
  local copies, waits for them, and re-layouts  5.78 us (7%)
    pallas_call x1, Pallas kernels, body(): pl.pallas_call(kernel, out_shape=(jax.ShapeDtypeStruct((TILE, H * HD), bf...  78.5 us
    unnamed x8, local copies, waits for them, and re-layouts  5.78 us

profile of v1, /device:TPU:1, one launch (start us, length us, event | category | flops | bytes accessed | tf_op | source)
XLA Modules:
  0.0 85.0 jit_solution(18444764730062573563)
XLA Ops:
  0.6 1.4 %copy.10.tiles = s32[64,4]{1,0:T(8,128)} copy(s32[64,4]{0,1:T(4,128)} %param.13) | data formatting | bytes 2048 | tf_op args[6]
  2.0 78.5 %shard_map.94 = (bf16[128,8192]{1,0:T(8,128)(2,1)}, f32[16,1024]{1,0:T(8,128)}, f32[16,1024]{1,0:T(8,128)}) custom-call(s32[4]{0:T(128)} %links.1, s32[4]{0:T(128)} %counts.1, s32[64,4]{1,0:T(8,128)} %copy.10.tiles, bf16[128,8192]{1,0:T(8,128)(2,1)} %q_hbm.1, bf16[128,8192]{1,0:T(8,128)(2,1)} %g_hbm.1, bf16[16,1024]{1,0:T(8,128)(2,1)} %k_in.1, ...), custom_call_target="tpu_custom_call" | custom-call | flops 7046430720 | bytes 8388608 | tf_op jit(solution)/shard_map/pallas_call | solution.py:417
  80.5 0.0 copy-start.1
  80.5 0.0 copy-start
  80.6 3.1 %copy.14 = bf16[128,8192]{1,0:T(8,128)(2,1)} copy(bf16[128,8192]{1,0:T(8,128)(2,1)} %get-tuple-element.6) | data formatting | bytes 4194304
  83.7 0.0 copy-done.1
  83.7 0.6 copy.15
  84.3 0.0 copy-done
  84.3 0.6 copy.16
Async XLA Ops:
  80.5 3.2 %copy-start.1 = (f32[16,1024]{1,0:T(8,128)S(1)}, f32[16,1024]{1,0:T(8,128)}, u32[]{:S(2)}) copy-start(f32[16,1024]{1,0:T(8,128)} %get-tuple-element.7) | copy-start | bytes 196612
  80.5 3.8 %copy-start = (f32[16,1024]{1,0:T(8,128)S(1)}, f32[16,1024]{1,0:T(8,128)}, u32[]{:S(2)}) copy-start(f32[16,1024]{1,0:T(8,128)} %get-tuple-element.8) | copy-start | bytes 196612

commit v2 on v1

--- a/solution.py
+++ b/solution.py
@@ -26,7 +26,10 @@
 SCALE = 1.0 / math.sqrt(HD)
 SCALE2 = SCALE * math.log2(math.e)
 NEG = -1e30
-Z_GROUPS = ((0, 1), (1, 3), (4, 4))
+HAND_STEPS = 4
+Z_FIRST = 5
+AHEAD = 4
+SPARE = KVH
 MESH = pl.DeviceIdType.MESH
 f32 = jnp.float32
 bf16 = jnp.bfloat16
@@ -56,7 +59,7 @@
     links, counts, tiles, q_hbm, g_hbm, k_in, v_in,
     dq_hbm, dk_out, dv_out,
     q, g, dq, kv, cur, kaug, vc, kt, s0, s1, d0, d1, e_buf, p0, p1, w0, w1, dk_acc, dv_acc,
-    rs_full, rs_sib, rs_y, rs_yr, rs_z, rs_zr, src_tbl, dst_tbl, row_tbl,
+    rs_full, rs_sib, rs_y, rs_yr, rs_z, rs_zr, sums, src_tbl, dst_tbl, row_tbl,
     load_sem, dq_sem, zs, zr, ys, yr, cs, cr, rcs, rcr, rys, ryr, rzs, rzr,
 ):
     c = lax.axis_index("context")
@@ -84,14 +87,11 @@
         kv[h, k, y, z, 1] = v_in[:, h * HD : (h + 1) * HD]
     pl.semaphore_wait(barrier, len(peers))
 
-    def z_send(group, d):
-        heads = pl.ds(*Z_GROUPS[group])
-        mine = kv.at[heads, k, y, z]
-        return remote(mine, mine, z_sem, (group, d - 1), z_peer[d])
-
-    def z_recv(group, d):
-        heads = pl.ds(*Z_GROUPS[group])
-        return remote(kv.at[heads, k, y, z], kv.at[heads, k, y, zz[NZ - d]], z_sem, (group, d - 1), z_peer[d])
+    def z_send(h, d):
+        return remote(kv.at[h, k, y, z], kv.at[h, k, y, z], z_sem, (h, d - 1), z_peer[d])
+
+    def z_recv(h, d):
+        return remote(kv.at[h, k, y, z], kv.at[h, k, y, zz[NZ - d]], z_sem, (h, d - 1), z_peer[d])
 
     def y_send(h, d):
         return remote(kv.at[h, k, y], kv.at[h, k, y], y_sem, (h, d - 1), y_peer[d])
@@ -105,63 +105,92 @@
     def c_recv(h):
         return remote(kv.at[h, k], kv.at[h, other], c_sem, (h,), sibling)
 
-    for group in range(len(Z_GROUPS)):
-        for d in range(1, NZ):
-            z_send(group, d).start()
-
-    def pass_on(group):
-        for d in range(1, NZ):
-            z_recv(group, d).wait_recv()
-        first, number = Z_GROUPS[group]
-        for h in range(first, first + number):
+    def block_send(h, d):
+        return remote(kv.at[h, k, y, z], kv.at[h, k, y, z], y_sem, (h, d - 1), y_peer[d])
+
+    def block_recv(h, d):
+        return remote(kv.at[h, k, y, z], kv.at[h, k, yy[NY - d], z], y_sem, (h, d - 1), y_peer[d])
+
+    def column_send(h, d):
+        return remote(kv.at[h, k, :, z], kv.at[h, k, :, z], z_sem, (h, d - 1), z_peer[d])
+
+    def column_recv(h, d):
+        return remote(kv.at[h, k, :, z], kv.at[h, k, :, zz[NZ - d]], z_sem, (h, d - 1), z_peer[d])
+
+    def start_column(h):
+        for d in range(1, NY):
+            block_recv(h, d).wait_recv()
+        for d in range(1, NZ):
+            column_send(h, d).start()
+
+    def start_y(h):
+        for d in range(1, NZ):
+            z_recv(h, d).wait_recv()
+        for d in range(1, NY):
+            y_send(h, d).start()
+
+    def start_c(h):
+        for d in range(1, NY):
+            y_recv(h, d).wait_recv()
+        c_send(h).start()
+
+    def start_c_late(h):
+        for d in range(1, NZ):
+            column_recv(h, d).wait_recv()
+        c_send(h).start()
+
+    for h in range(KVH):
+        if h < Z_FIRST:
+            for d in range(1, NZ):
+                z_send(h, d).start()
+        else:
             for d in range(1, NY):
-                y_send(h, d).start()
-
-    pass_on(0)
-
-    zero = jnp.int32(0)
-    live_rows, first_block = [], [zero]
-    for image in range(IMAGES):
-        seen = zero
-        for p in range(IMAGES):
-            seen = seen + jnp.where(links[p] == image, tiles[c, p], 0)
-        live_rows.append(jnp.where(seen > 0, counts[image], 0))
-        first_block.append(first_block[-1] + (live_rows[-1] + (ROWS - 1)) // ROWS)
-    spare = first_block[IMAGES]
-
-    def fill_src(b, _):
-        image, base, rows = zero, zero, live_rows[0]
-        for i in range(1, IMAGES):
-            past = b >= first_block[i]
-            image = jnp.where(past, i, image)
-            base = jnp.where(past, first_block[i], base)
-            rows = jnp.where(past, live_rows[i], rows)
-        u = jnp.minimum(b - base, VIS // ROWS - 1)
-        src_tbl[b] = lax.rem(u, 2) * (NY * NZ) + image * NZ + u // 2
-        row_tbl[b] = jnp.where(b < spare, rows - (b - base) * ROWS, 0)
-        return 0
-
-    lax.fori_loop(0, LIVE, fill_src, 0)
-    for image in range(IMAGES):
-
-        def fill_dst(u, _):
-            at = lax.rem(u, 2) * (NY * NZ) + image * NZ + u // 2
-            dst_tbl[at] = jnp.where(u * ROWS < live_rows[image], first_block[image] + u, LIVE)
+                block_send(h, d).start()
+
+    def prepare():
+        zero = jnp.int32(0)
+        live_rows, first_block = [], [zero]
+        for image in range(IMAGES):
+            seen = zero
+            for p in range(IMAGES):
+                seen = seen + jnp.where(links[p] == image, tiles[p, c], 0)
+            live_rows.append(jnp.where(seen > 0, counts[image], 0))
+            first_block.append(first_block[-1] + (live_rows[-1] + (ROWS - 1)) // ROWS)
+        spare = first_block[IMAGES]
+
+        def fill_src(b, _):
+            image, base, rows = zero, zero, live_rows[0]
+            for i in range(1, IMAGES):
+                past = b >= first_block[i]
+                image = jnp.where(past, i, image)
+                base = jnp.where(past, first_block[i], base)
+                rows = jnp.where(past, live_rows[i], rows)
+            u = jnp.minimum(b - base, VIS // ROWS - 1)
+            src_tbl[b] = lax.rem(u, 2) * (NY * NZ) + image * NZ + u // 2
+            row_tbl[b] = jnp.where(b < spare, rows - (b - base) * ROWS, 0)
             return 0
 
-        lax.fori_loop(0, VIS // ROWS, fill_dst, 0)
-
-    lane = lax.broadcasted_iota(jnp.int32, (ROWS, HD), 1)
-    row = lax.broadcasted_iota(jnp.int32, (ROWS, HD), 0)
-
-    def fill_bias(b, _):
-        dead = jnp.logical_and(lane == 0, row >= row_tbl[b])
-        kaug[b, :, HD:] = jnp.where(dead, NEG, 0.0).astype(bf16)
-        return 0
-
-    lax.fori_loop(0, LIVE, fill_bias, 0)
-    dk_acc[LIVE] = jnp.zeros((ROWS, HD), f32)
-    dv_acc[LIVE] = jnp.zeros((ROWS, HD), f32)
+        lax.fori_loop(0, LIVE, fill_src, 0)
+        for image in range(IMAGES):
+
+            def fill_dst(u, _):
+                at = lax.rem(u, 2) * (NY * NZ) + image * NZ + u // 2
+                dst_tbl[at] = jnp.where(u * ROWS < live_rows[image], first_block[image] + u, LIVE)
+                return 0
+
+            lax.fori_loop(0, VIS // ROWS, fill_dst, 0)
+
+        lane = lax.broadcasted_iota(jnp.int32, (ROWS, HD), 1)
+        row = lax.broadcasted_iota(jnp.int32, (ROWS, HD), 0)
+
+        def fill_bias(b, _):
+            dead = jnp.logical_and(lane == 0, row >= row_tbl[b])
+            kaug[b, :, HD:] = jnp.where(dead, NEG, 0.0).astype(bf16)
+            return 0
+
+        lax.fori_loop(0, LIVE, fill_bias, 0)
+        dk_acc[LIVE] = jnp.zeros((ROWS, HD), f32)
+        dv_acc[LIVE] = jnp.zeros((ROWS, HD), f32)
 
     def compact(h):
         flat = 2 * NY * NZ
@@ -237,122 +266,179 @@
         cols = pl.ds(pl.multiple_of(h * (GROUP * HD), GROUP * HD), GROUP * HD)
         return pltpu.make_async_copy(dq.at[:, cols], dq_hbm.at[:, cols], dq_sem.at[h])
 
-    def finish(h):
+    def finish(slot):
         for plane in range(2):
             for a in range(NY):
                 for b in range(NZ):
                     at = dst_tbl[plane * (NY * NZ) + a * NZ + b]
-                    rs_full[h, plane, a, b, 0] = (dk_acc[at] * SCALE).astype(bf16)
-                    rs_full[h, plane, a, b, 1] = dv_acc[at].astype(bf16)
+                    rs_full[slot, plane, a, b, 0] = (dk_acc[at] * SCALE).astype(bf16)
+                    rs_full[slot, plane, a, b, 1] = dv_acc[at].astype(bf16)
+
+    def start_rc(h):
         rc_send(h).start()
         dq_store(h).start()
 
-    def reduce_core(h):
-        rc_send(h).wait_recv()
+    def reduce_core(slot):
         for a in range(NY):
-            rs_y[h, a] = (rs_full[h, k, a].astype(f32) + rs_sib[h, a].astype(f32)).astype(bf16)
+            rs_y[slot, a] = (rs_full[slot, k, a].astype(f32) + rs_sib[slot, a].astype(f32)).astype(bf16)
+
+    def start_ry(h):
         for d in range(1, NY):
             ry_send(h, d).start()
 
-    def reduce_y(h):
-        total = rs_y[h, y].astype(f32)
+    def wait_ry(h):
         for d in range(1, NY):
             ry_send(h, d).wait_recv()
-            total = total + rs_yr[h, d - 1].astype(f32)
-        rs_z[h] = total.astype(bf16)
+
+    def reduce_y(slot):
+        total = rs_y[slot, y].astype(f32)
+        for d in range(1, NY):
+            total = total + rs_yr[slot, d - 1].astype(f32)
+        rs_z[slot] = total.astype(bf16)
+
+    def start_rz(h):
         for d in range(1, NZ):
             rz_send(h, d).start()
 
-    def reduce_z(h):
-        total = rs_z[h, z].astype(f32)
+    def wait_rz(h):
         for d in range(1, NZ):
             rz_send(h, d).wait_recv()
-            total = total + rs_zr[h, d - 1].astype(f32)
-        cols = pl.ds(pl.multiple_of(h * HD, HD), HD)
-        dk_out[:, cols] = total[0]
-        dv_out[:, cols] = total[1]
-
-    def bring(h):
-        for d in range(1, NY):
-            y_recv(h, d).wait_recv()
-        c_send(h).start()
-
-    bring(0)
-    pass_on(1)
+
+    def reduce_z(slot):
+        total = rs_z[slot, z].astype(f32)
+        for d in range(1, NZ):
+            total = total + rs_zr[slot, d - 1].astype(f32)
+        sums[slot] = total
+
+    for h in range(AHEAD):
+        start_y(h)
+        if h == 0:
+            prepare()
+    start_c(0)
+    for h in range(Z_FIRST, KVH):
+        start_column(h)
+    q_load.wait()
+    g_load.wait()
     c_recv(0).wait_recv()
     compact(0)
-    q_load.wait()
-    g_load.wait()
     front(0, 0, 0)
 
     def step(h, _):
+        def late(lag):
+            return jnp.where(h >= lag, h - lag, SPARE)
+
+        @pl.when(h < Z_FIRST - 1)
+        def _():
+            start_c(h + 1)
+
+        @pl.when(jnp.logical_and(h >= Z_FIRST - 1, h < KVH - 1))
+        def _():
+            start_c_late(h + 1)
+
+        @pl.when(h >= 2)
+        def _():
+            rc_send(h - 2).wait_recv()
+
+        @pl.when(h >= 4)
+        def _():
+            wait_ry(h - 4)
+
+        @pl.when(h >= 6)
+        def _():
+            wait_rz(h - 6)
+
         front(h, 1, 1)
         middle(0)
-
-        @pl.when(h == 0)
-        def _():
-            pass_on(2)
-
-        @pl.when(h > 0)
-        def _():
-            back(h - 1, 3, 1, False)
-            finish(h - 1)
-
-        @pl.when(h < KVH - 1)
-        def _():
-            bring(h + 1)
+        back(jnp.maximum(h - 1, 0), 3, 1, False)
+        finish(late(1))
+        reduce_core(late(2))
+        reduce_y(late(4))
+        reduce_z(late(6))
+
+        @pl.when(h < Z_FIRST - AHEAD)
+        def _():
+            start_y(h + AHEAD)
+
+        @pl.when(h >= 1)
+        def _():
+            start_rc(h - 1)
+
+        @pl.when(h >= 2)
+        def _():
+            start_ry(h - 2)
+
+        @pl.when(h >= 4)
+        def _():
+            start_rz(h - 4)
 
         transpose_keys()
         front(h, 2, 0)
         middle(1)
         back(h, 0, 0, True)
-
-        @pl.when(h >= 1)
-        def _():
-            reduce_core(h - 1)
-
         front(h, 3, 1)
         middle(0)
         back(h, 1, 1, False)
 
-        @pl.when(h >= 3)
-        def _():
-            reduce_y(h - 3)
-
-        @pl.when(h >= 5)
-        def _():
-            reduce_z(h - 5)
-
         @pl.when(h < KVH - 1)
         def _():
             c_recv(h + 1).wait_recv()
-            compact(h + 1)
-
+
+        compact(jnp.minimum(h + 1, KVH - 1))
         front(jnp.minimum(h + 1, KVH - 1), 0, 0)
         middle(1)
         back(h, 2, 0, False)
         return 0
 
     lax.fori_loop(0, KVH, step, 0)
-    back(KVH - 1, 3, 1, False)
-    finish(KVH - 1)
-    reduce_y(KVH - 3)
-    reduce_z(KVH - 5)
-    reduce_core(KVH - 1)
-    reduce_y(KVH - 2)
-    reduce_z(KVH - 4)
-    reduce_y(KVH - 1)
-    reduce_z(KVH - 3)
-    reduce_z(KVH - 2)
-    reduce_z(KVH - 1)
-
-    for group in range(len(Z_GROUPS)):
-        for d in range(1, NZ):
-            z_send(group, d).wait_send()
+    last = KVH - 1
+    rc_send(last - 1).wait_recv()
+    reduce_core(last - 1)
+    start_ry(last - 1)
+    back(last, 3, 1, False)
+    finish(last)
+    start_rc(last)
+    wait_ry(last - 3)
+    reduce_y(last - 3)
+    start_rz(last - 3)
+    rc_send(last).wait_recv()
+    reduce_core(last)
+    start_ry(last)
+    for h in (last - 2, last - 1):
+        wait_ry(h)
+        reduce_y(h)
+        start_rz(h)
+    for h in (last - 5, last - 4, last - 3, last - 2):
+        wait_rz(h)
+        reduce_z(h)
+    wait_ry(last)
+    reduce_y(last)
+    start_rz(last)
+    wait_rz(last - 1)
+    reduce_z(last - 1)
+    for h in range(last):
+        dk_out[:, h * HD : (h + 1) * HD] = sums[h, 0]
+        dv_out[:, h * HD : (h + 1) * HD] = sums[h, 1]
+    wait_rz(last)
+    reduce_z(last)
+    dk_out[:, last * HD :] = sums[last, 0]
+    dv_out[:, last * HD :] = sums[last, 1]
 
     def drain(h, _):
-        for d in range(1, NY):
-            y_send(h, d).wait_send()
+        @pl.when(h < Z_FIRST)
+        def _():
+            for d in range(1, NZ):
+                z_send(h, d).wait_send()
+            for d in range(1, NY):
+                y_send(h, d).wait_send()
+
+        @pl.when(h >= Z_FIRST)
+        def _():
+            for d in range(1, NZ):
+                column_send(h, d).wait_send()
+            for d in range(1, NY):
+                block_send(h, d).wait_send()
+
+        for d in range(1, NY):
             ry_send(h, d).wait_send()
         for d in range(1, NZ):
             rz_send(h, d).wait_send()
@@ -362,6 +448,15 @@
         return 0
 
     lax.fori_loop(0, KVH, drain, 0)
+
+
+def hand_out(dq, dk, dv, dq_out, dk_out, dv_out):
+    dq_out[...] = dq[...]
+
+    @pl.when(pl.program_id(0) == 0)
+    def _():
+        dk_out[...] = dk[...]
+        dv_out[...] = dv[...]
 
 
 def body(queries, out_grad, image_keys, image_values, link_ids, token_counts, tile_mask):
@@ -390,19 +485,20 @@
         pltpu.VMEM((L, lanes), bf16),
         pltpu.VMEM((LIVE + 1, ROWS, HD), f32),
         pltpu.VMEM((LIVE + 1, ROWS, HD), f32),
-        pltpu.VMEM((KVH, 2, NY, NZ, 2, ROWS, HD), bf16),
-        pltpu.VMEM((KVH, NY, NZ, 2, ROWS, HD), bf16),
-        pltpu.VMEM((KVH, NY, NZ, 2, ROWS, HD), bf16),
-        pltpu.VMEM((KVH, NY - 1, NZ, 2, ROWS, HD), bf16),
-        pltpu.VMEM((KVH, NZ, 2, ROWS, HD), bf16),
-        pltpu.VMEM((KVH, NZ - 1, 2, ROWS, HD), bf16),
+        pltpu.VMEM((KVH + 1, 2, NY, NZ, 2, ROWS, HD), bf16),
+        pltpu.VMEM((KVH + 1, NY, NZ, 2, ROWS, HD), bf16),
+        pltpu.VMEM((KVH + 1, NY, NZ, 2, ROWS, HD), bf16),
+        pltpu.VMEM((KVH + 1, NY - 1, NZ, 2, ROWS, HD), bf16),
+        pltpu.VMEM((KVH + 1, NZ, 2, ROWS, HD), bf16),
+        pltpu.VMEM((KVH + 1, NZ - 1, 2, ROWS, HD), bf16),
+        pltpu.VMEM((KVH + 1, 2, ROWS, HD), f32),
         pltpu.SMEM((LIVE,), jnp.int32),
         pltpu.SMEM((BLOCKS,), jnp.int32),
         pltpu.SMEM((LIVE,), jnp.int32),
         dma((2,)),
         dma((KVH,)),
-        dma((len(Z_GROUPS), NZ - 1)),
-        dma((len(Z_GROUPS), NZ - 1)),
+        dma((KVH, NZ - 1)),
+        dma((KVH, NZ - 1)),
         dma((KVH, NY - 1)),
         dma((KVH, NY - 1)),
         dma((KVH,)),
@@ -414,7 +510,7 @@
         dma((KVH, NZ - 1)),
         dma((KVH, NZ - 1)),
     ]
-    return pl.pallas_call(
+    results = pl.pallas_call(
         kernel,
         out_shape=(
             jax.ShapeDtypeStruct((TILE, H * HD), bf16),
@@ -430,7 +526,17 @@
         cost_estimate=pl.CostEstimate(
             flops=5 * 2 * TILE * H * L * HD, bytes_accessed=8 << 20, transcendentals=TILE * H * L
         ),
-    )(link_ids, token_counts, tile_mask, queries, out_grad, image_keys, image_values)
+    )(link_ids, token_counts, tile_mask.T, queries, out_grad, image_keys, image_values)
+    wide = pl.BlockSpec((TILE, H * HD // HAND_STEPS), lambda i: (0, i))
+    whole = pl.BlockSpec((ROWS, KVH * HD), lambda i: (0, 0))
+    specs = [wide, whole, whole]
+    return pl.pallas_call(
+        hand_out,
+        out_shape=tuple(jax.ShapeDtypeStruct(r.shape, r.dtype) for r in results),
+        grid=(HAND_STEPS,),
+        in_specs=specs,
+        out_specs=specs,
+    )(*results)
 
 
 def solution(mesh):

time: 85.2 us -> 72.4 us (0.85)
  Pallas kernels: 78.5 us -> 71.5 us
  local copies, waits for them, and re-layouts: 5.78 us -> 0 us
    pallas_call x1, Pallas kernels: 78.5 us -> 67.7 us  [body(): pl.pallas_call(kernel, out_shape=(jax.ShapeDtypeStruct((TILE, H * HD), bf...]
    unnamed x8 -> x0, local copies, waits for them, and re-layouts: 5.78 us -> none
    pallas_call x0 -> x1, Pallas kernels: none -> 3.84 us  [body(): pl.pallas_call(hand_out, out_shape=tuple((jax.ShapeDtypeStruct(r.shape, r...]
where the time goes in v2:
time: 72.4 us; the launch traced here: 72.1 us
  Pallas kernels  71.5 us (99%)
    pallas_call x1, Pallas kernels, body(): pl.pallas_call(kernel, out_shape=(jax.ShapeDtypeStruct((TILE, H * HD), bf...  67.7 us
    pallas_call x1, Pallas kernels, body(): pl.pallas_call(hand_out, out_shape=tuple((jax.ShapeDtypeStruct(r.shape, r...  3.84 us

profile of v2, /device:TPU:1, one launch (start us, length us, event | category | flops | bytes accessed | tf_op | source)
XLA Modules:
  0.0 72.1 jit_solution(10730459204161194249)
XLA Ops:
  0.6 67.7 %shard_map.94 = (bf16[128,8192]{1,0:T(8,128)(2,1)}, f32[16,1024]{1,0:T(8,128)}, f32[16,1024]{1,0:T(8,128)}) custom-call(s32[4]{0:T(128)} %links.1, s32[4]{0:T(128)} %counts.1, s32[4,64]{1,0:T(4,128)} %bitcast.1, bf16[128,8192]{1,0:T(8,128)(2,1)} %q_hbm.1, bf16[128,8192]{1,0:T(8,128)(2,1)} %g_hbm.1, bf16[16,1024]{1,0:T(8,128)(2,1)} %k_in.1, bf16[16,1024]{1,0:T(8,128)(2,1)} %v_in.1), custom_call_target="tpu_custom_call" | custom-call | flops 7046430720 | bytes 8388608 | tf_op jit(solution)/shard_map/pallas_call | solution.py:513
  68.3 3.8 %shard_map.95 = (bf16[128,8192]{1,0:T(8,128)(2,1)}, f32[16,1024]{1,0:T(8,128)}, f32[16,1024]{1,0:T(8,128)}) custom-call(bf16[128,8192]{1,0:T(8,128)(2,1)} %get-tuple-element.6.dq, f32[16,1024]{1,0:T(8,128)} %get-tuple-element.7.dk, f32[16,1024]{1,0:T(8,128)} %get-tuple-element.8.dv), custom_call_target="tpu_custom_call" | custom-call | tf_op jit(solution)/shard_map/pallas_call | solution.py:533

commit v3 on v2

--- a/solution.py
+++ b/solution.py
@@ -26,7 +26,7 @@
 SCALE = 1.0 / math.sqrt(HD)
 SCALE2 = SCALE * math.log2(math.e)
 NEG = -1e30
-HAND_STEPS = 4
+HAND_STEPS = 8
 Z_FIRST = 5
 AHEAD = 4
 SPARE = KVH
@@ -199,8 +199,8 @@
             kaug[b, :, :HD] = cur[src_tbl[b], 0]
             vc[b] = cur[src_tbl[b], 1]
 
-    def transpose_keys():
-        kt[...] = kaug[...].reshape(L, 2 * HD)[:, :HD].T
+    def transpose_keys(h):
+        kt[h] = kaug[...].reshape(L, 2 * HD)[:, :HD].T
 
     s_buf, d_buf, p_buf, w_buf = (s0, s1), (d0, d1), (p0, p1), (w0, w1)
     ones = jnp.where(lax.broadcasted_iota(jnp.int32, (2 * TILE, HD), 1) == 0, 1.0, 0.0).astype(bf16)
@@ -215,7 +215,8 @@
         s_buf[slot][...] = dot(kaug[...].reshape(L, 2 * HD), rows_q, 1, 1)
         d_buf[slot][...] = dot(vc[...].reshape(L, HD), two_heads(g, h, pair), 1, 1)
 
-    def middle(slot):
+    def middle(h, pair):
+        slot, to = pair % 2, h * 2 + pair // 2
         tops, sums, deltas = [], [], []
         lanes = 2 * TILE
         for i in range(L // CHUNK):
@@ -237,15 +238,26 @@
             at = slice(i * CHUNK, (i + 1) * CHUNK)
             prob = e_buf[at, :] * (weight[i] * inverse)
             p_buf[slot][at, :] = prob.astype(bf16)
-            w_buf[slot][at, :] = (prob * (d_buf[slot][at, :] - delta)).astype(bf16)
-
-    def back(h, pair, slot, first):
-        dqt = dot(kt[...], w_buf[slot][...], 1, 0) * SCALE
+            w_buf[slot][to, at, :] = (prob * (d_buf[slot][at, :] - delta)).astype(bf16)
+
+    def query_terms(h, pair):
+        dqt = dot(kt[h], w_buf[pair % 2][h * 2 + pair // 2], 1, 0) * SCALE
         for j in range(2):
             start = pl.multiple_of(h * (GROUP * HD) + pair * (2 * HD) + j * HD, HD)
             dq[:, pl.ds(start, HD)] = dqt[:, j * TILE : (j + 1) * TILE].T.astype(bf16)
+
+    def query_grads(first, number):
+        def one(h, _):
+            for pair in range(PAIRS):
+                query_terms(h, pair)
+            dq_store(h).start()
+            return 0
+
+        lax.fori_loop(first, first + number, one, 0)
+
+    def back(h, pair, slot, first):
         dv = dot(p_buf[slot][...], two_heads(g, h, pair), 1, 0).reshape(LIVE, ROWS, HD)
-        dk = dot(w_buf[slot][...], two_heads(q, h, pair), 1, 0).reshape(LIVE, ROWS, HD)
+        dk = dot(w_buf[slot][h * 2 + pair // 2], two_heads(q, h, pair), 1, 0).reshape(LIVE, ROWS, HD)
         if first:
             dv_acc[:LIVE] = dv
             dk_acc[:LIVE] = dk
@@ -276,7 +288,6 @@
 
     def start_rc(h):
         rc_send(h).start()
-        dq_store(h).start()
 
     def reduce_core(slot):
         for a in range(NY):
@@ -310,10 +321,9 @@
             total = total + rs_zr[slot, d - 1].astype(f32)
         sums[slot] = total
 
+    prepare()
     for h in range(AHEAD):
         start_y(h)
-        if h == 0:
-            prepare()
     start_c(0)
     for h in range(Z_FIRST, KVH):
         start_column(h)
@@ -348,7 +358,7 @@
             wait_rz(h - 6)
 
         front(h, 1, 1)
-        middle(0)
+        middle(h, 0)
         back(jnp.maximum(h - 1, 0), 3, 1, False)
         finish(late(1))
         reduce_core(late(2))
@@ -371,12 +381,12 @@
         def _():
             start_rz(h - 4)
 
-        transpose_keys()
+        transpose_keys(h)
         front(h, 2, 0)
-        middle(1)
+        middle(h, 1)
         back(h, 0, 0, True)
         front(h, 3, 1)
-        middle(0)
+        middle(h, 2)
         back(h, 1, 1, False)
 
         @pl.when(h < KVH - 1)
@@ -385,7 +395,7 @@
 
         compact(jnp.minimum(h + 1, KVH - 1))
         front(jnp.minimum(h + 1, KVH - 1), 0, 0)
-        middle(1)
+        middle(h, 3)
         back(h, 2, 0, False)
         return 0
 
@@ -403,16 +413,19 @@
     rc_send(last).wait_recv()
     reduce_core(last)
     start_ry(last)
+    query_grads(0, 3)
     for h in (last - 2, last - 1):
         wait_ry(h)
         reduce_y(h)
         start_rz(h)
+    query_grads(3, 2)
     for h in (last - 5, last - 4, last - 3, last - 2):
         wait_rz(h)
         reduce_z(h)
     wait_ry(last)
     reduce_y(last)
     start_rz(last)
+    query_grads(5, 3)
     wait_rz(last - 1)
     reduce_z(last - 1)
     for h in range(last):
@@ -450,13 +463,20 @@
     lax.fori_loop(0, KVH, drain, 0)
 
 
-def hand_out(dq, dk, dv, dq_out, dk_out, dv_out):
-    dq_out[...] = dq[...]
-
-    @pl.when(pl.program_id(0) == 0)
-    def _():
-        dk_out[...] = dk[...]
-        dv_out[...] = dv[...]
+def hand_out(dq, dk, dv, dq_out, dk_out, dv_out, dq_mid, dk_mid, dv_mid, sems):
+    width = H * HD // HAND_STEPS
+    steps = [pl.ds(i * width, width) for i in range(HAND_STEPS)]
+    parts = [(dk, dk_mid, dk_out), (dv, dv_mid, dv_out)]
+    parts += [(dq.at[:, at], dq_mid.at[:, at], dq_out.at[:, at]) for at in steps]
+    reads = [pltpu.make_async_copy(a, b, sems.at[0, i]) for i, (a, b, _) in enumerate(parts)]
+    writes = [pltpu.make_async_copy(b, c, sems.at[1, i]) for i, (_, b, c) in enumerate(parts)]
+    for copy in reads:
+        copy.start()
+    for read, write in zip(reads, writes):
+        read.wait()
+        write.start()
+    for copy in writes:
+        copy.wait()
 
 
 def body(queries, out_grad, image_keys, image_values, link_ids, token_counts, tile_mask):
@@ -473,7 +493,7 @@
         pltpu.VMEM((BLOCKS, 2, ROWS, HD), bf16),
         pltpu.VMEM((LIVE, ROWS, 2 * HD), bf16),
         pltpu.VMEM((LIVE, ROWS, HD), bf16),
-        pltpu.VMEM((HD, L), bf16),
+        pltpu.VMEM((KVH, HD, L), bf16),
         pltpu.VMEM((L, lanes), f32),
         pltpu.VMEM((L, lanes), f32),
         pltpu.VMEM((L, lanes), f32),
@@ -481,8 +501,8 @@
         pltpu.VMEM((L, lanes), f32),
         pltpu.VMEM((L, lanes), bf16),
         pltpu.VMEM((L, lanes), bf16),
-        pltpu.VMEM((L, lanes), bf16),
-        pltpu.VMEM((L, lanes), bf16),
+        pltpu.VMEM((KVH * PAIRS // 2, L, lanes), bf16),
+        pltpu.VMEM((KVH * PAIRS // 2, L, lanes), bf16),
         pltpu.VMEM((LIVE + 1, ROWS, HD), f32),
         pltpu.VMEM((LIVE + 1, ROWS, HD), f32),
         pltpu.VMEM((KVH + 1, 2, NY, NZ, 2, ROWS, HD), bf16),
@@ -527,15 +547,12 @@
             flops=5 * 2 * TILE * H * L * HD, bytes_accessed=8 << 20, transcendentals=TILE * H * L
         ),
     )(link_ids, token_counts, tile_mask.T, queries, out_grad, image_keys, image_values)
-    wide = pl.BlockSpec((TILE, H * HD // HAND_STEPS), lambda i: (0, i))
-    whole = pl.BlockSpec((ROWS, KVH * HD), lambda i: (0, 0))
-    specs = [wide, whole, whole]
     return pl.pallas_call(
         hand_out,
         out_shape=tuple(jax.ShapeDtypeStruct(r.shape, r.dtype) for r in results),
-        grid=(HAND_STEPS,),
-        in_specs=specs,
-        out_specs=specs,
+        in_specs=[hbm] * 3,
+        out_specs=[hbm] * 3,
+        scratch_shapes=[pltpu.VMEM(r.shape, r.dtype) for r in results] + [dma((2, HAND_STEPS + 2))],
     )(*results)
 
 

time: 72.4 us -> 69.7 us (0.963)
  Pallas kernels: 71.5 us -> 68.6 us
    pallas_call x1, Pallas kernels: 67.7 us -> 66.1 us  [body(): pl.pallas_call(kernel, out_shape=(jax.ShapeDtypeStruct((TILE, H * HD), bf...]
    pallas_call x1, Pallas kernels: 3.84 us -> 2.51 us  [body(): pl.pallas_call(hand_out, out_shape=tuple((jax.ShapeDtypeStruct(r.shape, r...]
where the time goes in v3:
time: 69.7 us; the launch traced here: 69.3 us
  Pallas kernels  68.6 us (98%)
    pallas_call x1, Pallas kernels, body(): pl.pallas_call(kernel, out_shape=(jax.ShapeDtypeStruct((TILE, H * HD), bf...  66.1 us
    pallas_call x1, Pallas kernels, body(): pl.pallas_call(hand_out, out_shape=tuple((jax.ShapeDtypeStruct(r.shape, r...  2.51 us

profile of v3, /device:TPU:1, one launch (start us, length us, event | category | flops | bytes accessed | tf_op | source)
XLA Modules:
  0.0 69.3 jit_solution(996041675328417759)
XLA Ops:
  0.6 66.1 %shard_map.94 = (bf16[128,8192]{1,0:T(8,128)(2,1)}, f32[16,1024]{1,0:T(8,128)}, f32[16,1024]{1,0:T(8,128)}) custom-call(s32[4]{0:T(128)} %links.1, s32[4]{0:T(128)} %counts.1, s32[4,64]{1,0:T(4,128)} %bitcast.1, bf16[128,8192]{1,0:T(8,128)(2,1)} %q_hbm.1, bf16[128,8192]{1,0:T(8,128)(2,1)} %g_hbm.1, bf16[16,1024]{1,0:T(8,128)(2,1)} %k_in.1, bf16[16,1024]{1,0:T(8,128)(2,1)} %v_in.1), custom_call_target="tpu_custom_call" | custom-call | flops 7046430720 | bytes 8388608 | tf_op jit(solution)/shard_map/pallas_call | solution.py:533
  66.8 2.5 %shard_map.95 = (bf16[128,8192]{1,0:T(8,128)(2,1)}, f32[16,1024]{1,0:T(8,128)}, f32[16,1024]{1,0:T(8,128)}) custom-call(bf16[128,8192]{1,0:T(8,128)(2,1)} %get-tuple-element.6.dq, f32[16,1024]{1,0:T(8,128)} %get-tuple-element.7.dk, f32[16,1024]{1,0:T(8,128)} %get-tuple-element.8.dv), custom_call_target="tpu_custom_call" | custom-call | tf_op jit(solution)/shard_map/pallas_call | solution.py:550

commit v4 on v3

--- a/solution.py
+++ b/solution.py
@@ -60,7 +60,7 @@
     dq_hbm, dk_out, dv_out,
     q, g, dq, kv, cur, kaug, vc, kt, s0, s1, d0, d1, e_buf, p0, p1, w0, w1, dk_acc, dv_acc,
     rs_full, rs_sib, rs_y, rs_yr, rs_z, rs_zr, sums, src_tbl, dst_tbl, row_tbl,
-    load_sem, dq_sem, zs, zr, ys, yr, cs, cr, rcs, rcr, rys, ryr, rzs, rzr,
+    load_sem, dq_sem, ws, wr, zs, zr, ys, yr, cs, cr, rcs, rcr, rys, ryr, rzs, rzr,
 ):
     c = lax.axis_index("context")
     y, z, k = c // (2 * NZ), lax.rem(c // 2, NZ), lax.rem(c, 2)
@@ -70,7 +70,7 @@
     sibling = device(y, z, other)
     y_peer = [device(yy[d], z, k) for d in range(NY)]
     z_peer = [device(y, zz[d], k) for d in range(NZ)]
-    z_sem, y_sem, c_sem = (zs, zr), (ys, yr), (cs, cr)
+    z_sem, y_sem, c_sem, row_sem = (zs, zr), (ys, yr), (cs, cr), (ws, wr)
     rc_sem, ry_sem, rz_sem = (rcs, rcr), (rys, ryr), (rzs, rzr)
 
     q_load = pltpu.make_async_copy(q_hbm, q, load_sem.at[0])
@@ -101,6 +101,13 @@
 
     def c_send(h):
         return remote(kv.at[h, k], kv.at[h, k], c_sem, (h,), sibling)
+
+    def row_send(d):
+        row = kv.at[0, k, yy[d]]
+        return remote(row, row, row_sem, (d,), sibling)
+
+    def row_recv(d):
+        return remote(kv.at[0, k, yy[d]], kv.at[0, other, yy[d]], row_sem, (d,), sibling)
 
     def c_recv(h):
         return remote(kv.at[h, k], kv.at[h, other], c_sem, (h,), sibling)
@@ -322,14 +329,19 @@
         sums[slot] = total
 
     prepare()
-    for h in range(AHEAD):
-        start_y(h)
-    start_c(0)
+    start_y(0)
+    row_send(0).start()
     for h in range(Z_FIRST, KVH):
         start_column(h)
+    for h in range(1, AHEAD):
+        start_y(h)
+    for d in (1, 3, 2):
+        y_recv(0, d).wait_recv()
+        row_send(NY - d).start()
     q_load.wait()
     g_load.wait()
-    c_recv(0).wait_recv()
+    for d in range(NY):
+        row_recv(d).wait_recv()
     compact(0)
     front(0, 0, 0)
 
@@ -349,21 +361,16 @@
         def _():
             rc_send(h - 2).wait_recv()
 
-        @pl.when(h >= 4)
-        def _():
-            wait_ry(h - 4)
-
-        @pl.when(h >= 6)
-        def _():
-            wait_rz(h - 6)
+        @pl.when(h >= 5)
+        def _():
+            wait_ry(h - 5)
 
         front(h, 1, 1)
         middle(h, 0)
         back(jnp.maximum(h - 1, 0), 3, 1, False)
         finish(late(1))
         reduce_core(late(2))
-        reduce_y(late(4))
-        reduce_z(late(6))
+        reduce_y(late(5))
 
         @pl.when(h < Z_FIRST - AHEAD)
         def _():
@@ -377,9 +384,9 @@
         def _():
             start_ry(h - 2)
 
-        @pl.when(h >= 4)
-        def _():
-            start_rz(h - 4)
+        @pl.when(h >= 5)
+        def _():
+            start_rz(h - 5)
 
         transpose_keys(h)
         front(h, 2, 0)
@@ -407,9 +414,10 @@
     back(last, 3, 1, False)
     finish(last)
     start_rc(last)
-    wait_ry(last - 3)
-    reduce_y(last - 3)
-    start_rz(last - 3)
+    for h in (last - 4, last - 3):
+        wait_ry(h)
+        reduce_y(h)
+        start_rz(h)
     rc_send(last).wait_recv()
     reduce_core(last)
     start_ry(last)
@@ -419,15 +427,16 @@
         reduce_y(h)
         start_rz(h)
     query_grads(3, 2)
-    for h in (last - 5, last - 4, last - 3, last - 2):
+    for h in range(last - 2):
         wait_rz(h)
         reduce_z(h)
     wait_ry(last)
     reduce_y(last)
     start_rz(last)
     query_grads(5, 3)
-    wait_rz(last - 1)
-    reduce_z(last - 1)
+    for h in (last - 2, last - 1):
+        wait_rz(h)
+        reduce_z(h)
     for h in range(last):
         dk_out[:, h * HD : (h + 1) * HD] = sums[h, 0]
         dv_out[:, h * HD : (h + 1) * HD] = sums[h, 1]
@@ -455,12 +464,17 @@
             ry_send(h, d).wait_send()
         for d in range(1, NZ):
             rz_send(h, d).wait_send()
-        c_send(h).wait_send()
+        @pl.when(h > 0)
+        def _():
+            c_send(h).wait_send()
+
         rc_send(h).wait_send()
         dq_store(h).wait()
         return 0
 
     lax.fori_loop(0, KVH, drain, 0)
+    for d in range(NY):
+        row_send(d).wait_send()
 
 
 def hand_out(dq, dk, dv, dq_out, dk_out, dv_out, dq_mid, dk_mid, dv_mid, sems):
@@ -517,6 +531,8 @@
         pltpu.SMEM((LIVE,), jnp.int32),
         dma((2,)),
         dma((KVH,)),
+        dma((NY,)),
+        dma((NY,)),
         dma((KVH, NZ - 1)),
         dma((KVH, NZ - 1)),
         dma((KVH, NY - 1)),

time: 69.7 us -> 69.5 us (level)
  no operation moved by 1% of the time
where the time goes in v4:
time: 69.5 us; the launch traced here: 69 us
  Pallas kernels  68.3 us (98%)
    pallas_call x1, Pallas kernels, body(): pl.pallas_call(kernel, out_shape=(jax.ShapeDtypeStruct((TILE, H * HD), bf...  65.8 us
    pallas_call x1, Pallas kernels, body(): pl.pallas_call(hand_out, out_shape=tuple((jax.ShapeDtypeStruct(r.shape, r...  2.51 us

profile of v4, /device:TPU:1, one launch (start us, length us, event | category | flops | bytes accessed | tf_op | source)
XLA Modules:
  0.0 69.0 jit_solution(15732784314285742917)
XLA Ops:
  0.6 65.8 %shard_map.94 = (bf16[128,8192]{1,0:T(8,128)(2,1)}, f32[16,1024]{1,0:T(8,128)}, f32[16,1024]{1,0:T(8,128)}) custom-call(s32[4]{0:T(128)} %links.1, s32[4]{0:T(128)} %counts.1, s32[4,64]{1,0:T(4,128)} %bitcast.1, bf16[128,8192]{1,0:T(8,128)(2,1)} %q_hbm.1, bf16[128,8192]{1,0:T(8,128)(2,1)} %g_hbm.1, bf16[16,1024]{1,0:T(8,128)(2,1)} %k_in.1, bf16[16,1024]{1,0:T(8,128)(2,1)} %v_in.1), custom_call_target="tpu_custom_call" | custom-call | flops 7046430720 | bytes 8388608 | tf_op jit(solution)/shard_map/pallas_call | solution.py:549
  66.5 2.5 %shard_map.95 = (bf16[128,8192]{1,0:T(8,128)(2,1)}, f32[16,1024]{1,0:T(8,128)}, f32[16,1024]{1,0:T(8,128)}) custom-call(bf16[128,8192]{1,0:T(8,128)(2,1)} %get-tuple-element.6.dq, f32[16,1024]{1,0:T(8,128)} %get-tuple-element.7.dk, f32[16,1024]{1,0:T(8,128)} %get-tuple-element.8.dv), custom_call_target="tpu_custom_call" | custom-call | tf_op jit(solution)/shard_map/pallas_call | solution.py:566
